TPU v7x, 32 devices: a whole 2x2x4 slice. The times are simulated.
32 devices in a mesh: dp: 4 (over y, x), ctx: 8 (over z, core).
Axes of the slice: x: 2, y: 2, z: 4, core: 2. Of those that a mesh axis runs over, the one named last changes fastest.
Arguments:
- queries: bfloat16 [4, 1024, 1280], P('dp', 'ctx'), may hold values from -16 to 16
- keys: bfloat16 [4, 1024, 1280], P('dp', 'ctx'), may hold values from -16 to 16
- values: bfloat16 [4, 1024, 1280], P('dp', 'ctx'), may hold values from -6 to 6
- seg_lengths: int32 [4, 8], P('dp'), may hold values from 1 to 768, 1024 in all within a row
- out_grad: bfloat16 [4, 1024, 2560], P('dp', 'ctx'), may hold values from -6 to 6
- w_out: bfloat16 [1280, 2560], P('dp'), may hold values from -0.15625 to 0.15625
Outputs:
- attended: bfloat16 [4, 1024, 2560], P('dp', 'ctx')
- query_grad: bfloat16 [4, 1024, 1280], P('dp', 'ctx')
- key_grad: bfloat16 [4, 1024, 1280], P('dp', 'ctx')
- value_grad: bfloat16 [4, 1024, 1280], P('dp', 'ctx')
- w_out_grad: float32 [1280, 2560], P('dp')
Inputs may be any that keep to these rules, and one draw needn't show every extreme that they name: `seg_lengths`: each record's lengths sum to 1024; the longest of each record is exactly 768.
All inputs are finite; a program needn't handle non-finite values.
Results may differ from a plain program's by a relative error of at most 0.027.
Values may be sent and summed in bfloat16 or wider, within the bound.
A program may use at most 192 MiB of HBM per device.

v0:
```python
import math

import jax
import jax.numpy as jnp
from jax import lax
from jax.sharding import PartitionSpec as P

HEADS = 10
HD = 128


MASKED_SCORE = -1e30


def segment_ids(length_row, row_total):
    segment_ends = jnp.cumsum(length_row)
    positions = lax.iota(jnp.int32, row_total)
    return jnp.sum((segment_ends[None, :] <= positions[:, None]).astype(jnp.int32), axis=1)


def head_columns(matrix, head_index, head_width):
    return lax.dynamic_slice_in_dim(matrix, head_index * head_width, head_width, 1)


def take_rows(matrix, first_row, row_count):
    return lax.dynamic_slice_in_dim(matrix, first_row, row_count, 0)


def contract_last(left_side, right_side):
    return lax.dot_general(
        left_side, right_side, (((1,), (1,)), ((), ())), preferred_element_type=jnp.float32
    )


def contract_first(left_side, right_side):
    return lax.dot_general(
        left_side, right_side, (((0,), (0,)), ((), ())), preferred_element_type=jnp.float32
    )


def attend_forward(
    local_query, all_key, all_value, local_segments, all_segments, block_rows, score_scale
):
    local_rows = local_query.shape[0]
    all_rows = all_key.shape[0]
    block_count = all_rows // block_rows

    def one_head(head_index, carried):
        attention, log_norm, stored = carried
        query_head = head_columns(local_query, head_index, HD)
        key_head = head_columns(all_key, head_index, HD)
        value_head = head_columns(all_value, head_index, HD)
        head_scores = contract_last(query_head, key_head) * score_scale

        def block_scores(first_row):
            key_segments = take_rows(all_segments, first_row, block_rows)
            scores = lax.dynamic_slice_in_dim(head_scores, first_row, block_rows, 1)
            return (scores, local_segments[:, None] == key_segments[None, :])

        def stat_step(block_index, running):
            first_row = block_index * block_rows
            row_max, row_sum = running
            scores, same_segment = block_scores(first_row)
            new_max = jnp.maximum(
                row_max, jnp.max(jnp.where(same_segment, scores, MASKED_SCORE), axis=1)
            )
            shifted = jnp.where(same_segment, jnp.exp(scores - new_max[:, None]), 0.0)
            return (new_max, row_sum * jnp.exp(row_max - new_max) + jnp.sum(shifted, axis=1))

        start_state = (
            jnp.full((local_rows,), MASKED_SCORE, jnp.float32),
            jnp.zeros((local_rows,), jnp.float32),
        )
        row_max, row_sum = lax.fori_loop(0, block_count, stat_step, start_state)
        head_norm = row_max + jnp.log(row_sum)

        def value_step(block_index, accumulated):
            first_row = block_index * block_rows
            scores, same_segment = block_scores(first_row)
            soft_weights = jnp.where(
                same_segment, jnp.exp(scores - head_norm[:, None]), 0.0
            ).astype(jnp.bfloat16)
            value_block = take_rows(value_head, first_row, block_rows)
            return accumulated + jnp.dot(
                soft_weights, value_block, preferred_element_type=jnp.float32
            )

        summed = lax.fori_loop(0, block_count, value_step, jnp.zeros((local_rows, HD), jnp.float32))
        attention = lax.dynamic_update_slice_in_dim(
            attention, summed.astype(jnp.bfloat16), head_index * HD, 1
        )
        log_norm = lax.dynamic_update_slice_in_dim(log_norm, head_norm[:, None], head_index, 1)
        stored = lax.dynamic_update_slice_in_dim(stored, head_scores[None], head_index, 0)
        return (attention, log_norm, stored)

    start_triple = (
        jnp.zeros((local_rows, HEADS * HD), jnp.bfloat16),
        jnp.zeros((local_rows, HEADS), jnp.float32),
        jnp.zeros((HEADS, local_rows, all_rows), jnp.float32),
    )
    return lax.fori_loop(0, HEADS, one_head, start_triple)


def attend_backward(
    local_query,
    local_key,
    local_value,
    local_grad,
    local_norm,
    local_dot,
    all_query,
    all_key,
    all_value,
    all_grad,
    all_norm,
    all_dot,
    local_segments,
    all_segments,
    stored,
    block_rows,
    score_scale,
):
    local_rows = local_query.shape[0]
    block_count = all_key.shape[0] // block_rows

    def one_head(head_index, carried):
        query_grad, key_grad, value_grad = carried
        grad_head = head_columns(local_grad, head_index, HD)
        own_key = head_columns(local_key, head_index, HD)
        own_value = head_columns(local_value, head_index, HD)
        key_head = head_columns(all_key, head_index, HD)
        value_head = head_columns(all_value, head_index, HD)
        query_all = head_columns(all_query, head_index, HD)
        grad_all = head_columns(all_grad, head_index, HD)
        norm_head = head_columns(local_norm, head_index, 1)[:, 0]
        dot_head = head_columns(local_dot, head_index, 1)[:, 0]
        norm_all = head_columns(all_norm, head_index, 1)[:, 0]
        dot_all = head_columns(all_dot, head_index, 1)[:, 0]
        head_scores = lax.dynamic_index_in_dim(stored, head_index, 0, keepdims=False)

        def query_step(block_index, accumulated):
            first_row = block_index * block_rows
            key_segments = take_rows(all_segments, first_row, block_rows)
            key_block = take_rows(key_head, first_row, block_rows)
            value_block = take_rows(value_head, first_row, block_rows)
            scores = lax.dynamic_slice_in_dim(head_scores, first_row, block_rows, 1)
            same_segment = local_segments[:, None] == key_segments[None, :]
            probs = jnp.where(same_segment, jnp.exp(scores - norm_head[:, None]), 0.0)
            dprob = contract_last(grad_head, value_block)
            dscore = (probs * (dprob - dot_head[:, None])).astype(jnp.bfloat16)
            return accumulated + jnp.dot(dscore, key_block, preferred_element_type=jnp.float32)

        query_sum = lax.fori_loop(
            0, block_count, query_step, jnp.zeros((local_rows, HD), jnp.float32)
        )

        def key_step(block_index, running):
            first_row = block_index * block_rows
            query_segments = take_rows(all_segments, first_row, block_rows)
            key_sum, value_sum = running
            query_block = take_rows(query_all, first_row, block_rows)
            grad_block = take_rows(grad_all, first_row, block_rows)
            norm_block = take_rows(norm_all, first_row, block_rows)
            dot_block = take_rows(dot_all, first_row, block_rows)
            scores = contract_last(query_block, own_key) * score_scale
            same_segment = query_segments[:, None] == local_segments[None, :]
            probs = jnp.where(same_segment, jnp.exp(scores - norm_block[:, None]), 0.0)
            dprob = contract_last(grad_block, own_value)
            dscore = (probs * (dprob - dot_block[:, None])).astype(jnp.bfloat16)
            key_sum = key_sum + contract_first(dscore, query_block)
            value_sum = value_sum + contract_first(probs.astype(jnp.bfloat16), grad_block)
            return (key_sum, value_sum)

        zeros = jnp.zeros((local_rows, HD), jnp.float32)
        key_sum, value_sum = lax.fori_loop(0, block_count, key_step, (zeros, zeros))
        query_grad = lax.dynamic_update_slice_in_dim(
            query_grad, (query_sum * score_scale).astype(jnp.bfloat16), head_index * HD, 1
        )
        key_grad = lax.dynamic_update_slice_in_dim(
            key_grad, (key_sum * score_scale).astype(jnp.bfloat16), head_index * HD, 1
        )
        value_grad = lax.dynamic_update_slice_in_dim(
            value_grad, value_sum.astype(jnp.bfloat16), head_index * HD, 1
        )
        return (query_grad, key_grad, value_grad)

    empty = jnp.zeros((local_rows, HEADS * HD), jnp.bfloat16)
    return lax.fori_loop(0, HEADS, one_head, (empty, empty, empty))


def local(queries, keys, values, seg_lengths, out_grad, w_out):
    score_scale = 1.0 / math.sqrt(HD)
    local_rows = queries.shape[1]
    all_rows = local_rows * lax.axis_size("ctx")
    block_rows = min(all_rows, 512)
    local_query = queries[0]
    local_key = keys[0]
    local_value = values[0]
    local_outgrad = out_grad[0]
    all_segments = segment_ids(seg_lengths[0], all_rows)
    local_segments = take_rows(all_segments, lax.axis_index("ctx") * local_rows, local_rows)
    full_weight = lax.all_gather(w_out, "dp", axis=0, tiled=True)
    attn_grad = contract_last(local_outgrad, full_weight).astype(jnp.bfloat16)
    all_key, all_value, all_query, all_grad = (
        lax.all_gather(local_key, "ctx", axis=0, tiled=True),
        lax.all_gather(local_value, "ctx", axis=0, tiled=True),
        lax.all_gather(local_query, "ctx", axis=0, tiled=True),
        lax.all_gather(attn_grad, "ctx", axis=0, tiled=True),
    )
    attention, log_norm, stored = attend_forward(
        local_query, all_key, all_value, local_segments, all_segments, block_rows, score_scale
    )
    attended = jnp.dot(attention, full_weight, preferred_element_type=jnp.float32).astype(
        jnp.bfloat16
    )
    products = attn_grad.astype(jnp.float32) * attention.astype(jnp.float32)
    grad_dot = jnp.sum(products.reshape(local_rows, HEADS, HD), axis=2)
    all_norm, all_dot = (
        lax.all_gather(log_norm, "ctx", axis=0, tiled=True),
        lax.all_gather(grad_dot, "ctx", axis=0, tiled=True),
    )
    query_grad, key_grad, value_grad = attend_backward(
        local_query,
        local_key,
        local_value,
        attn_grad,
        log_norm,
        grad_dot,
        all_query,
        all_key,
        all_value,
        all_grad,
        all_norm,
        all_dot,
        local_segments,
        all_segments,
        stored,
        block_rows,
        score_scale,
    )
    grad_share = lax.psum_scatter(
        contract_first(attention, local_outgrad).astype(jnp.bfloat16),
        "dp",
        scatter_dimension=0,
        tiled=True,
    )
    weight_grad = lax.psum(grad_share, "ctx").astype(jnp.float32)
    return (attended[None], query_grad[None], key_grad[None], value_grad[None], weight_grad)


def solution(mesh):
    in_specs = (
        P("dp", "ctx", None),
        P("dp", "ctx", None),
        P("dp", "ctx", None),
        P("dp", None),
        P("dp", "ctx", None),
        P("dp", None),
    )
    out_specs = (
        P("dp", "ctx", None),
        P("dp", "ctx", None),
        P("dp", "ctx", None),
        P("dp", "ctx", None),
        P("dp", None),
    )
    return jax.shard_map(local, mesh=mesh, in_specs=in_specs, out_specs=out_specs, check_vma=False)
```

profile of v0, /device:TPU:17, one launch (start us, length us, event | category | flops | bytes accessed | tf_op | source)
XLA Modules:
  0.0 419.1 jit_solution(8447683285333391024)
XLA Ops:
  10.5 33.6 %all-gather.13.cloned.1.call-done = bf16[1,1024,1280]{2,1,0:T(8,128)(2,1)} async-done(((bf16[1,128,1280]{2,1,0:T(8,128)(2,1)}), bf16[1,1024,1280]{2,1,0:T(8,128)(2,1)}) %all-gather.13.cloned.1.call-update) | async-done | bytes 2621456 | tf_op jit(solution)/shard_map/all_gather | solution.py:205
  44.0 34.5 %all-gather.15.cloned.1.call-done = bf16[1,1024,1280]{2,1,0:T(8,128)(2,1)} async-done(((bf16[1,128,1280]{2,1,0:T(8,128)(2,1)}), bf16[1,1024,1280]{2,1,0:T(8,128)(2,1)}) %all-gather.15.cloned.1.call-update) | async-done | bytes 2621456 | tf_op jit(solution)/shard_map/all_gather | solution.py:206
  78.6 48.8 %while.152 = (s32[]{:T(128)}, bf16[128,1280]{1,0:T(8,128)(2,1)S(1)}, f32[128,10]{0,1:T(8,128)S(1)}, f32[10,128,1024]{2,1,0:T(8,128)}, bf16[128,1280]{1,0:T(8,128...) while((s32[]{:T(128)}, bf16[128,1280]{1,0:T(8,128)(2,1)S(1)}, ...), condition=%wide.region_9.10_spmd, body=%wide.region_2.9_spmd.sunk | while | flops 51233556 | bytes 3044121 | solution.py:101
  78.6 2.0 bitcast_dynamic-update-slice_fusion.2
  83.5 2.0 bitcast_dynamic-update-slice_fusion.2
  88.4 2.0 bitcast_dynamic-update-slice_fusion.2
  98.2 2.0 bitcast_dynamic-update-slice_fusion.2
  103.0 2.0 bitcast_dynamic-update-slice_fusion.2
  107.9 2.0 bitcast_dynamic-update-slice_fusion.2
  112.8 2.0 bitcast_dynamic-update-slice_fusion.2
  122.6 2.0 bitcast_dynamic-update-slice_fusion.2
  127.5 4.6 %convolution_convert_fusion = bf16[1280,2560]{1,0:T(8,128)(2,1)} fusion(bf16[128,1280]{1,0:T(8,128)(2,1)S(1)} %get-tuple-element.1124, bf16[1,128,2560]{2,1,0:T(8,128)(2,1)S(1)} %copy-done), kind=kOutput, calls=%fused_computation.82 | convolution fusion | flops 842137600 | bytes 7536640 | tf_op jit(solution)/shard_map/dot_general | solution.py:36
  132.7 19.8 %all-gather.9.cloned.1.call-done = bf16[1280,2560]{1,0:T(8,128)(2,1)} async-done(((bf16[320,2560]{1,0:T(8,128)(2,1)}), bf16[1280,2560]{1,0:T(8,128)(2,1)}) %all-gather.9.cloned.1.call-update) | async-done | bytes 6553616 | tf_op jit(solution)/shard_map/all_gather | solution.py:202
  152.5 5.8 %convert_multiply_fusion = (f32[128,1280]{1,0:T(8,128)S(1)}, bf16[128,1280]{1,0:T(8,128)(2,1)}) fusion(bf16[128,1280]{1,0:T(8,128)(2,1)S(1)} %get-tuple-element.1124, bf16[1280,2560]{1,0:T(8,128)(2,1)} %all-gather.9.cloned.1.call-done, bf16[1,128,2560]{2,1,0:T(8,128)(2,1)S(1)} %copy-done), kind=kOutput, calls=%fused_computation.88 | convolution fusion | flops 839516160 | bytes 8519680 | tf_op jit(solution)/shard_map/dot_general | solution.py:30
  158.4 12.6 %all_gather.26 = f32[1024,10]{0,1:T(8,128)S(1)} all-gather(f32[128,10]{0,1:T(8,128)S(1)} %get-tuple-element.2072), channel_id=1, replica_groups=mesh['dp'=4,'ctx'=8] {'ctx'}, dimensions={0}, use_global_device_ids=true | all-gather | bytes 46080 | tf_op jit(solution)/shard_map/all_gather | solution.py:219
  171.3 13.9 %all_gather.27 = f32[1024,10]{0,1:T(8,128)S(1)} all-gather(f32[128,10]{0,1:T(8,128)S(1)} %reduce_sum.32), channel_id=1, replica_groups=mesh['dp'=4,'ctx'=8] {'ctx'}, dimensions={0}, use_global_device_ids=true | all-gather | bytes 46080 | tf_op jit(solution)/shard_map/all_gather | solution.py:220
  185.2 4.8 %fusion.56 = bf16[1,128,2560]{2,1,0:T(8,128)(2,1)} fusion(bf16[128,1280]{1,0:T(8,128)(2,1)S(1)} %get-tuple-element.1124, bf16[1280,2560]{1,0:T(8,128)(2,1)} %all-gather.9.cloned.1.call-done), kind=kOutput, calls=%fused_computation.84 | convolution fusion | flops 839188480 | bytes 7536640 | tf_op jit(solution)/shard_map/dot_general | solution.py:213
  190.0 37.8 %reduce-scatter.2.cloned.1.call-done = bf16[320,2560]{1,0:T(8,128)(2,1)} async-done(((bf16[1280,2560]{1,0:T(8,128)(2,1)}), bf16[320,2560]{1,0:T(8,128)(2,1)}) %reduce-scatter.2.cloned.1.call-update) | async-done | bytes 1638416 | tf_op jit(solution)/shard_map/reduce_scatter | solution.py:241
  227.8 34.8 %all-gather.17.cloned.1.call-done = bf16[1,1024,1280]{2,1,0:T(8,128)(2,1)} async-done(((bf16[1,128,1280]{2,1,0:T(8,128)(2,1)}), bf16[1,1024,1280]{2,1,0:T(8,128)(2,1)}) %all-gather.17.cloned.1.call-update) | async-done | bytes 2621456 | tf_op jit(solution)/shard_map/all_gather | solution.py:207
  262.6 35.0 %all-gather.11.cloned.1.call-done = bf16[1024,1280]{1,0:T(8,128)(2,1)} async-done(((bf16[128,1280]{1,0:T(8,128)(2,1)}), bf16[1024,1280]{1,0:T(8,128)(2,1)}) %all-gather.11.cloned.1.call-update) | async-done | bytes 2621456 | tf_op jit(solution)/shard_map/all_gather | solution.py:208
  297.7 110.6 %while.155 = (s32[]{:T(128)}, bf16[128,1280]{1,0:T(8,128)(2,1)S(1)}, bf16[128,1280]{1,0:T(8,128)(2,1)S(1)}, bf16[128,1280]{1,0:T(8,128)(2,1)S(1)}, bf16[1024,128...) while((s32[]{:T(128)}, bf16[128,1280]{1,0:T(8,128)(2,1)S(1)}, ...), condition=%wide.region_16.17_spmd, body=%wide.region_11.16_spmd.sunk | while | flops 101761040 | bytes 7062036 | solution.py:188
  306.3 2.3 while.159
  317.4 2.3 while.159
  328.5 2.3 while.159
  339.5 2.3 while.159
  350.6 2.3 while.159
  361.7 2.3 while.159
  372.7 2.3 while.159
  383.8 2.3 while.159
  394.8 2.3 while.159
  405.9 2.3 while.159
  408.4 3.8 convert_element_type.83
  (636 shorter events, 171.0 us)
Async XLA Ops:
  7.2 120.3 %copy-start = (bf16[1,128,2560]{2,1,0:T(8,128)(2,1)S(1)}, bf16[1,128,2560]{2,1,0:T(8,128)(2,1)}, u32[]{:S(2)}) copy-start(bf16[1,128,2560]{2,1,0:T(8,128)(2,1)} %param.22) | copy-start | bytes 1966084
  7.2 36.9 %all-gather.13.cloned.1.call-start = ((), (), s32[]{:S(2)}) async-start(), calls=%async_computation.5 | async-start | bytes 2949120 | tf_op jit(solution)/shard_map/all_gather | solution.py:205
  7.9 70.7 %all-gather.15.cloned.1.call-start = ((), (), s32[]{:S(2)}) async-start(), calls=%async_computation.6 | async-start | bytes 2949120 | tf_op jit(solution)/shard_map/all_gather | solution.py:206
  8.7 143.9 %all-gather.9.cloned.1.call-start = ((), (), s32[]{:S(2)}) async-start(), calls=%async_computation.1 | async-start | bytes 8192000 | tf_op jit(solution)/shard_map/all_gather | solution.py:202
  9.4 218.4 %reduce-scatter.2.cloned.1.call-start = ((), (), s32[]{:S(2)}) async-start(), calls=%async_computation.3 | async-start | bytes 8192000 | tf_op jit(solution)/shard_map/reduce_scatter | solution.py:241
  132.1 130.5 %all-gather.17.cloned.1.call-start = ((), (), s32[]{:S(2)}) async-start(), calls=%async_computation.7 | async-start | bytes 2949120 | tf_op jit(solution)/shard_map/all_gather | solution.py:207
  132.7 164.9 %all-gather.11.cloned.1.call-start = ((), (), s32[]{:S(2)}) async-start(), calls=%async_computation.2 | async-start | bytes 2949120 | tf_op jit(solution)/shard_map/all_gather | solution.py:208
  158.3 250.0 %all-reduce.2.cloned.1.call-start = ((), (), s32[]{:S(2)}) async-start(), calls=%async_computation.4 | async-start | bytes 3276800 | tf_op jit(solution)/shard_map/psum | solution.py:247
  408.3 3.9 copy-start.1
  408.3 3.9 copy-start.2
  408.3 3.9 copy-start.3
Sparse Core Ops, SparseCore 0:
  9.7 34.3 all-gather.12
  45.7 32.8 all-gather.14
  80.4 72.0 all-gather.8
  155.4 72.3 reduce-scatter.1
  229.3 33.2 all-gather.16
  264.7 32.8 all-gather.10
  299.9 58.6 all-reduce.1
where the time goes:
time: 426 us; the launch traced here: 419 us
  waiting for transfers between devices  198 us (46%)
  local copies, waits for them, and re-layouts  95 us (22%)
  matrix products  66.7 us (16%)
  blocking collectives  26.5 us (6%)
  between operations  14.3 us (3%)
  other arithmetic  13.7 us (3%)
  loops' own time  4.53 us (1%)
    dynamic_slice x120, local copies, waits for them, and re-layouts, head_columns(): lax.dynamic_slice_in_dim(matrix, head_index * head_width, head_width, 1)  72.2 us
    reduce_scatter x1, waiting for transfers between devices, local(): lax.psum_scatter(contract_first(attention, local_outgrad).astype(jnp.bflo...  37.8 us
    all_gather x1, waiting for transfers between devices, local(): lax.all_gather(attn_grad, 'ctx', axis=0, tiled=True)  35 us
    all_gather x1, waiting for transfers between devices, local(): lax.all_gather(local_query, 'ctx', axis=0, tiled=True)  34.8 us
    all_gather x1, waiting for transfers between devices, local(): lax.all_gather(local_value, 'ctx', axis=0, tiled=True)  34.5 us
    all_gather x1, waiting for transfers between devices, local(): lax.all_gather(local_key, 'ctx', axis=0, tiled=True)  33.6 us
    dot_general x31, matrix products, contract_last(): lax.dot_general(left_side, right_side, (((1,), (1,)), ((), ())), preferre...  30.5 us
    all_gather x1, waiting for transfers between devices, local(): full_weight = lax.all_gather(w_out, 'dp', axis=0, tiled=True)  19.8 us
  transfers between devices with their start and end apart: 7, of which 6 were waited for; matrix products, arithmetic and copies ran while one was open for 41% of the time, Pallas kernels for 0%

commit v1 on v0

v1 whole, which is shorter than its diff:
```python
import functools
import math

import jax
import jax.numpy as jnp
from jax import lax
from jax.experimental import pallas as pl
from jax.experimental.pallas import tpu as pltpu
from jax.sharding import PartitionSpec as P

HEADS = 10
HD = 128
MASKED_SCORE = -1e30
MESH = pl.DeviceIdType.MESH
BF16 = jnp.bfloat16
F32 = jnp.float32
VMEM_BYTES = 56 * 1024 * 1024


def owner_of(head, n):
    slot, place = divmod(head, n)
    if slot and 2 * place + 2 < n:
        place = 2 * place + 2
    return place, slot


def head_in_slot(me, slot, n):
    if slot == 0:
        return me, me < HEADS
    head, valid = 0, False
    for h in range(slot * n, min(HEADS, (slot + 1) * n)):
        place = owner_of(h, n)[0]
        head = jnp.where(me == place, h, head)
        valid = jnp.logical_or(valid, me == place)
    return head, valid


def dot_nt(a, b):
    return lax.dot_general(a, b, (((1,), (1,)), ((), ())), preferred_element_type=F32)


def dot_tn(a, b):
    return lax.dot_general(a, b, (((0,), (0,)), ((), ())), preferred_element_type=F32)


def dot_nn(a, b):
    return jnp.dot(a, b, preferred_element_type=F32)


def remote(src, dst, send, recv, dp, ctx):
    return pltpu.make_async_remote_copy(
        src_ref=src, dst_ref=dst, send_sem=send, recv_sem=recv, device_id=(dp, ctx), device_id_type=MESH
    )


def greet(n, ndp):
    me, dp = lax.axis_index("ctx"), lax.axis_index("dp")
    barrier = pltpu.get_barrier_semaphore()
    for step in range(1, n):
        pl.semaphore_signal(barrier, inc=1, device_id=(dp, lax.rem(me + step, n)), device_id_type=MESH)
    for step in range(1, ndp):
        pl.semaphore_signal(barrier, inc=1, device_id=(lax.rem(dp + step, ndp), me), device_id_type=MESH)
    pl.semaphore_wait(barrier, n - 1 + ndp - 1)


def scatter_kernel(
    n, ndp, q_ref, k_ref, v_ref, og_ref, w_ref, heads_ref, full_ref, grad_ref,
    send_sem, recv_sem, wsend, wrecv, fsend, frecv,
):
    me, dp = lax.axis_index("ctx"), lax.axis_index("dp")
    core = lax.rem(me, 2)
    sibling = me + 1 - 2 * core
    rows = q_ref.shape[0]
    wrows = w_ref.shape[0]
    half = wrows // 2
    greet(n, ndp)
    my_rows = pl.ds(pl.multiple_of(me * rows, rows), rows)

    def weight_rows(owner, which):
        return pl.ds(pl.multiple_of(owner * wrows + which * half, 16), half)

    weight_copies = []
    for step in range(1, ndp):
        copy = remote(
            w_ref.at[pl.ds(pl.multiple_of(core * half, 16), half)],
            full_ref.at[weight_rows(dp, core)],
            wsend.at[step], wrecv.at[step], lax.rem(dp + step, ndp), me,
        )
        copy.start()
        weight_copies.append(copy)

    def send_head(tensor, source, head, start):
        place, slot = owner_of(head, n)
        columns = pl.ds(head * HD, HD)
        copy = remote(
            source.at[:, columns], heads_ref.at[slot, tensor, my_rows],
            send_sem.at[tensor, head], recv_sem.at[slot, tensor], dp, place,
        )

        @pl.when(me != place)
        def _():
            if start:
                copy.start()
            else:
                copy.wait_send()

        if start:
            @pl.when(me == place)
            def _():
                heads_ref[slot, tensor, my_rows, :] = source[:, columns]

    for tensor, source in enumerate((q_ref, k_ref, v_ref)):
        for head in range(HEADS):
            send_head(tensor, source, head, True)

    full_ref[pl.ds(pl.multiple_of(dp * wrows, 16), wrows), :] = w_ref[...]
    passes = []
    for step in range(1, ndp):
        weight_copies[step - 1].wait_recv()
        source = lax.rem(dp - step + ndp, ndp)
        block = full_ref.at[weight_rows(source, core)]
        copy = remote(block, block, fsend.at[step], frecv.at[step], dp, sibling)
        copy.start()
        passes.append(copy)
    for copy in passes:
        copy.wait_recv()
    for head in range(HEADS):
        columns = pl.ds(head * HD, HD)
        grad_ref[:, columns] = dot_nt(og_ref[...], full_ref[columns, :]).astype(BF16)
        send_head(3, grad_ref, head, True)

    for tensor, source in enumerate((q_ref, k_ref, v_ref, grad_ref)):
        for head in range(HEADS):
            send_head(tensor, source, head, False)
    for copy in weight_copies + passes:
        copy.wait_send()
    slots = heads_ref.shape[0]
    for slot in range(slots):
        @pl.when(head_in_slot(me, slot, n)[1])
        def _():
            for tensor in range(4):
                waited = heads_ref.at[slot, tensor, pl.ds(0, rows * (n - 1))]
                pltpu.make_async_copy(waited, waited, recv_sem.at[slot, tensor]).wait()


def attention_kernel(n, block, heads_ref, seg_col_ref, seg_row_ref, out_ref, key_sum, value_sum):
    me = lax.axis_index("ctx")
    scale = 1.0 / math.sqrt(HD)
    slots, _, seq, _ = heads_ref.shape
    for slot in range(slots):
        @pl.when(head_in_slot(me, slot, n)[1])
        def _():
            key_sum[...] = jnp.zeros_like(key_sum)
            value_sum[...] = jnp.zeros_like(value_sum)

            @pl.loop(0, seq // block)
            def _(index):
                rows = pl.ds(pl.multiple_of(index * block, block), block)
                query, grad = heads_ref[slot, 0, rows, :], heads_ref[slot, 3, rows, :]
                key, value = heads_ref[slot, 1], heads_ref[slot, 2]
                seen = seg_col_ref[rows, :] == seg_row_ref[...]
                scores = jnp.where(seen, dot_nt(query, key) * scale, MASKED_SCORE)
                top = jnp.max(scores, axis=1, keepdims=True)
                shifted = jnp.exp(scores - top)
                probs = shifted * (1.0 / jnp.sum(shifted, axis=1, keepdims=True))
                probs_b = probs.astype(BF16)
                attention = dot_nn(probs_b, value).astype(BF16)
                out_ref[slot, 0, rows, :] = attention
                grad_dot = jnp.sum(grad.astype(F32) * attention.astype(F32), axis=1, keepdims=True)
                dscore = (probs * (dot_nt(grad, value) - grad_dot)).astype(BF16)
                out_ref[slot, 1, rows, :] = (dot_nn(dscore, key) * scale).astype(BF16)
                key_sum[...] += dot_tn(dscore, query)
                value_sum[...] += dot_tn(probs_b, grad)

            out_ref[slot, 2] = (key_sum[...] * scale).astype(BF16)
            out_ref[slot, 3] = value_sum[...].astype(BF16)


def home_kernel(
    n, ndp, parts, heads_ref, full_ref, og_ref,
    attended_ref, qg_ref, kg_ref, vg_ref, wg_ref,
    att_ref, att_t, xsend_buf, xrecv_buf, csum, rbuf, hsum, zbuf, final,
    hsend, hrecv, xsend, xrecv, rsend, rrecv, zsend, zrecv, bsend, brecv, fsend, frecv,
):
    me, dp = lax.axis_index("ctx"), lax.axis_index("dp")
    core = lax.rem(me, 2)
    chip = me // 2
    sibling = me + 1 - 2 * core
    slots, _, seq, _ = heads_ref.shape
    rows = seq // n
    width = og_ref.shape[1]
    half = csum.shape[1]
    wide = width // parts
    tile = 512
    greet(n, ndp)
    targets = (att_ref, qg_ref, kg_ref, vg_ref)

    def home_copy(slot, tensor, step):
        head, valid = head_in_slot(me, slot, n)
        other = lax.rem(me + step, n)
        columns = pl.ds(pl.multiple_of(head * HD, HD), HD)
        source = heads_ref.at[slot, tensor, pl.ds(pl.multiple_of(other * rows, rows), rows)]
        return valid, remote(
            source, targets[tensor].at[:, columns],
            hsend.at[tensor, slot, step], hrecv.at[tensor, head], dp, other,
        )

    def send_home(tensor):
        for slot in range(slots):
            head, valid = head_in_slot(me, slot, n)

            @pl.when(valid)
            def _():
                for step in range(1, n):
                    home_copy(slot, tensor, step)[1].start()
                columns = pl.ds(pl.multiple_of(head * HD, HD), HD)
                mine = pl.ds(pl.multiple_of(me * rows, rows), rows)
                targets[tensor][:, columns] = heads_ref[slot, tensor, mine, :]

    def receive_home(tensor):
        for head in range(HEADS):
            place, _ = owner_of(head, n)

            @pl.when(me != place)
            def _():
                block = targets[tensor].at[:, pl.ds(head * HD, HD)]
                remote(block, block, hsend.at[tensor, 0, 0], hrecv.at[tensor, head], dp, place).wait_recv()

    for tensor in range(4):
        send_home(tensor)
    receive_home(0)

    att_t[...] = att_ref[...].T

    def share(owner, which):
        return pl.multiple_of(owner * 2 * half + which * half, 16)

    sib_copies = []
    for step in range(ndp):
        owner = lax.rem(dp + step + 1, ndp)
        left = att_t[pl.ds(share(owner, 1 - core), half), :]

        @pl.loop(0, width // tile)
        def _(index):
            columns = pl.ds(pl.multiple_of(index * tile, tile), tile)
            xsend_buf[step, :, columns] = dot_nn(left, og_ref[:, columns]).astype(BF16)

        copy = remote(xsend_buf.at[step], xrecv_buf.at[step], xsend.at[step], xrecv.at[step], dp, sibling)
        copy.start()
        sib_copies.append(copy)
    dp_copies = []
    for step in range(ndp):
        owner = lax.rem(dp + step + 1, ndp)
        left = att_t[pl.ds(share(owner, core), half), :]
        sib_copies[step].wait_recv()

        @pl.loop(0, width // tile)
        def _(index):
            columns = pl.ds(pl.multiple_of(index * tile, tile), tile)
            total = dot_nn(left, og_ref[:, columns]) + xrecv_buf[step, :, columns].astype(F32)
            csum[step, :, columns] = total.astype(BF16)

        if step < ndp - 1:
            copy = remote(csum.at[step], rbuf.at[step], rsend.at[step], rrecv.at[step], owner, me)
            copy.start()
            dp_copies.append(copy)

    @pl.loop(0, width // tile)
    def _(index):
        columns = pl.ds(pl.multiple_of(index * tile, tile), tile)
        attended_ref[:, columns] = dot_nn(att_ref[...], full_ref[:, columns]).astype(BF16)

    for copy in dp_copies:
        copy.wait_recv()
    total = csum[ndp - 1].astype(F32)
    for step in range(ndp - 1):
        total = total + rbuf[step].astype(F32)
    hsum[...] = total.astype(BF16)

    def part_columns(part):
        return pl.ds(part * wide, wide)

    def sum_copy(part):
        return remote(
            hsum.at[:, part_columns(part)], zbuf.at[chip],
            zsend.at[part], zrecv.at[chip], dp, 2 * part + core,
        )

    for part in range(parts):
        @pl.when(chip != part)
        def _():
            sum_copy(part).start()

    chips = n // 2
    my_half = pl.ds(pl.multiple_of(core * half, 16), half)
    for part in range(parts):
        @pl.when(chip == part)
        def _():
            total = hsum[:, part_columns(part)].astype(F32)
            for other in range(chips):
                if other != part:
                    block = zbuf.at[other]
                    remote(block, block, zsend.at[0], zrecv.at[other], dp, 2 * other + core).wait_recv()
                    total = total + zbuf[other].astype(F32)
            block = final.at[my_half, part_columns(part)]
            final[my_half, part_columns(part)] = total.astype(BF16)
            for other in range(chips):
                if other != part:
                    remote(block, block, bsend.at[other], brecv.at[part], dp, 2 * other + core).start()

    def part_block(part):
        return final.at[my_half, part_columns(part)]

    for turn in range(parts):
        part = turn
        block = part_block(part)

        @pl.when(chip != part)
        def _():
            remote(block, block, bsend.at[0], brecv.at[part], dp, 2 * part + core).wait_recv()

        remote(block, block, fsend.at[part], frecv.at[part], dp, sibling).start()
    for part in range(parts):
        theirs = final.at[pl.ds(pl.multiple_of((1 - core) * half, 16), half), part_columns(part)]
        remote(theirs, theirs, fsend.at[part], frecv.at[part], dp, sibling).wait_recv()
    wg_ref[...] = final[...].astype(F32)

    for tensor in range(1, 4):
        receive_home(tensor)
    for slot in range(slots):
        @pl.when(head_in_slot(me, slot, n)[1])
        def _():
            for tensor in range(4):
                for step in range(1, n):
                    home_copy(slot, tensor, step)[1].wait_send()
    for copy in sib_copies + dp_copies:
        copy.wait_send()
    for part in range(parts):
        block = part_block(part)
        remote(block, block, fsend.at[part], frecv.at[part], dp, sibling).wait_send()

        @pl.when(chip != part)
        def _():
            sum_copy(part).wait_send()

        @pl.when(chip == part)
        def _():
            for other in range(chips):
                if other != part:
                    remote(block, block, bsend.at[other], brecv.at[part], dp, 2 * other + core).wait_send()


def segment_ids(length_row, row_total):
    order = lax.iota(jnp.int32, length_row.shape[0])
    segment_ends = jnp.sum(jnp.where(order[None, :] <= order[:, None], length_row[None, :], 0), axis=1)
    positions = lax.iota(jnp.int32, row_total)
    return jnp.sum((segment_ends[None, :] <= positions[:, None]).astype(jnp.int32), axis=1)


def vmem(count):
    return [pl.BlockSpec(memory_space=pltpu.VMEM)] * count


def local(queries, keys, values, seg_lengths, out_grad, w_out):
    n, ndp = lax.axis_size("ctx"), lax.axis_size("dp")
    rows, inner = queries.shape[1:]
    width = out_grad.shape[2]
    seq = rows * n
    wrows = w_out.shape[0]
    half = wrows // 2
    slots = -(-HEADS // n)
    parts = math.gcd(n // 2, width // 128)
    wide = width // parts
    shape = jax.ShapeDtypeStruct
    dma = pltpu.SemaphoreType.DMA
    heads, full = pl.pallas_call(
        functools.partial(scatter_kernel, n, ndp),
        out_shape=(shape((slots, 4, seq, HD), BF16), shape((inner, width), BF16)),
        in_specs=vmem(5),
        out_specs=tuple(vmem(2)),
        scratch_shapes=[
            pltpu.VMEM((rows, inner), BF16),
            dma((4, HEADS)), dma((slots, 4)), dma((ndp,)), dma((ndp,)), dma((ndp,)), dma((ndp,)),
        ],
        compiler_params=pltpu.CompilerParams(
            collective_id=0, has_side_effects=True, vmem_limit_bytes=VMEM_BYTES
        ),
    )(queries[0], keys[0], values[0], out_grad[0], w_out)

    segments = segment_ids(seg_lengths[0], seq)
    results = pl.pallas_call(
        functools.partial(attention_kernel, n, 256),
        out_shape=shape((slots, 4, seq, HD), BF16),
        in_specs=vmem(3),
        out_specs=vmem(1)[0],
        scratch_shapes=[pltpu.VMEM((seq, HD), F32), pltpu.VMEM((seq, HD), F32)],
        compiler_params=pltpu.CompilerParams(vmem_limit_bytes=VMEM_BYTES),
    )(heads, segments[:, None], segments[None, :])

    attended, query_grad, key_grad, value_grad, weight_grad = pl.pallas_call(
        functools.partial(home_kernel, n, ndp, parts),
        out_shape=(
            shape((rows, width), BF16), shape((rows, inner), BF16), shape((rows, inner), BF16),
            shape((rows, inner), BF16), shape((wrows, width), F32),
        ),
        in_specs=vmem(3),
        out_specs=tuple(vmem(5)),
        scratch_shapes=[
            pltpu.VMEM((rows, inner), BF16),
            pltpu.VMEM((inner, rows), BF16),
            pltpu.VMEM((ndp, half, width), BF16),
            pltpu.VMEM((ndp, half, width), BF16),
            pltpu.VMEM((ndp, half, width), BF16),
            pltpu.VMEM((ndp - 1, half, width), BF16),
            pltpu.VMEM((half, width), BF16),
            pltpu.VMEM((n // 2, half, wide), BF16),
            pltpu.VMEM((wrows, width), BF16),
            dma((4, slots, n)), dma((4, HEADS)), dma((ndp,)), dma((ndp,)), dma((ndp,)), dma((ndp,)),
            dma((parts,)), dma((n // 2,)), dma((n // 2,)), dma((parts,)), dma((parts,)), dma((parts,)),
        ],
        compiler_params=pltpu.CompilerParams(
            collective_id=1, has_side_effects=True, vmem_limit_bytes=VMEM_BYTES
        ),
    )(results, full, out_grad[0])
    return (attended[None], query_grad[None], key_grad[None], value_grad[None], weight_grad)


def solution(mesh):
    in_specs = (
        P("dp", "ctx", None),
        P("dp", "ctx", None),
        P("dp", "ctx", None),
        P("dp", None),
        P("dp", "ctx", None),
        P("dp", None),
    )
    out_specs = (
        P("dp", "ctx", None),
        P("dp", "ctx", None),
        P("dp", "ctx", None),
        P("dp", "ctx", None),
        P("dp", None),
    )
    return jax.shard_map(local, mesh=mesh, in_specs=in_specs, out_specs=out_specs, check_vma=False)
```

time: 426 us -> 201 us (0.47); the launches traced: 419 us -> 200 us
  waiting for transfers between devices: 198 us -> 0 us
  Pallas kernels: 0 us -> 189 us
  local copies, waits for them, and re-layouts: 95 us -> 10 us
  matrix products: 66.7 us -> 0 us
  blocking collectives: 26.5 us -> 0 us
  between operations: 14.3 us -> 0.68 us
  other arithmetic: 13.7 us -> 0.85 us
  loops' own time: 4.53 us -> 0 us
    pallas_call x0 -> x3, Pallas kernels: none -> 189 us  [the longest x1 123 us: local(): pl.pallas_call(functools.partial(home_kernel, n, ndp, parts), out_shape=(...]
    all_gather x5 -> x0, waiting for transfers between devices: 158 us -> none  [the longest x1 35 us: local(): lax.all_gather(attn_grad, 'ctx', axis=0, tiled=True)]
    dynamic_slice x261 -> x0, local copies, waits for them, and re-layouts: 94.2 us -> none  [the longest x120 72.2 us: head_columns(): lax.dynamic_slice_in_dim(matrix, head_index * head_width, head_width, 1)]
    dot_general x113 -> x0, matrix products: 66.7 us -> none  [the longest x31 30.5 us: contract_last(): lax.dot_general(left_side, right_side, (((1,), (1,)), ((), ())), preferre...]
    reduce_scatter x1 -> x0, waiting for transfers between devices: 37.8 us -> none  [local(): lax.psum_scatter(contract_first(attention, local_outgrad).astype(jnp.bflo...]
    all_gather x2 -> x0, blocking collectives: 26.5 us -> none  [the longest x1 13.9 us: local(): lax.all_gather(grad_dot, 'ctx', axis=0, tiled=True)]
    unnamed x8 -> x9, local copies, waits for them, and re-layouts: 0.03 us -> 8.98 us
    another operation x42 -> x0, loops' own time: 4.53 us -> none  [the longest x1 1.13 us: attend_backward(): return lax.fori_loop(0, HEADS, one_head, (empty, empty, empty))]
  transfers between devices with their start and end apart: 7 -> 0, of which waited for: 6 -> 0; matrix products, arithmetic and copies ran while one was open for 41% -> 0% of each run, Pallas kernels for 0% -> 0%
where the time goes in v1:
time: 201 us; the launch traced here: 200 us
  Pallas kernels  189 us (94%)
  local copies, waits for them, and re-layouts  10 us (5%)
    pallas_call x1, Pallas kernels, local(): pl.pallas_call(functools.partial(home_kernel, n, ndp, parts), out_shape=(...  123 us
    pallas_call x1, Pallas kernels, local(): pl.pallas_call(functools.partial(scatter_kernel, n, ndp), out_shape=(shap...  57.5 us
    unnamed x9, local copies, waits for them, and re-layouts  8.98 us
    pallas_call x1, Pallas kernels, local(): pl.pallas_call(functools.partial(attention_kernel, n, 256), out_shape=sha...  8.7 us

profile of v1, /device:TPU:17, one launch (start us, length us, event | category | flops | bytes accessed | tf_op | source)
XLA Modules:
  0.0 200.3 jit_solution(6595044502337177675)
XLA Ops:
  0.6 0.8 select_reduce_fusion
  1.4 0.1 convert_reduce_fusion
  1.5 0.0 copy-start.1
  1.5 1.0 copy.12.seg_col_ref
  2.5 57.5 %shard_map.101 = (bf16[2,4,1024,128]{3,2,1,0:T(8,128)(2,1)}, bf16[1280,2560]{1,0:T(8,128)(2,1)}) custom-call(bf16[128,1280]{1,0:T(8,128)(2,1)} %bitcast.14, bf16[128,1280]{1,0:T(8,128)(2,1)} %bitcast.15, bf16[128,1280]{1,0:T(8,128)(2,1)} %bitcast.16, bf16[128,2560]{1,0:T(8,128)(2,1)} %bitcast.11, bf16[320,2560]{1,0:T(8,128)(2,1)} %w_ref.1), custom_call_target="tpu_custom_call" | custom-call | tf_op jit(solution)/shard_map/pallas_call | solution.py:376
  60.1 0.0 copy-done.1
  60.1 8.7 %shard_map.102.heads_ref = bf16[2,4,1024,128]{3,2,1,0:T(8,128)(2,1)} custom-call(bf16[2,4,1024,128]{3,2,1,0:T(8,128)(2,1)} %get-tuple-element.12.heads_ref, s32[1024,1]{1,0:T(8,128)} %copy.12.seg_col_ref, s32[1,1024]{1,0:T(1,128)} %bitcast.21), custom_call_target="tpu_custom_call" | custom-call | tf_op jit(solution)/shard_map/pallas_call | solution.py:391
  68.8 122.5 %shard_map.103 = (bf16[128,2560]{1,0:T(8,128)(2,1)}, bf16[128,1280]{1,0:T(8,128)(2,1)}, bf16[128,1280]{1,0:T(8,128)(2,1)}, bf16[128,1280]{1,0:T(8,128)(2,1)}, f32[320,2560]{1,0:T(8,128)}) custom-call(bf16[2,4,1024,128]{3,2,1,0:T(8,128)(2,1)} %shard_map.102.heads_ref, bf16[1280,2560]{1,0:T(8,128)(2,1)} %get-tuple-element.13.full_ref, bf16[128,2560]{1,0:T(8,128)(2,1)} %bitcast.12), custom_call_target="tpu_custom_call" | custom-call | tf_op jit(solution)/shard_map/pallas_call | solution.py:400
  191.3 0.0 copy-start
  191.3 2.1 %copy.18 = bf16[1,128,2560]{2,1,0:T(8,128)(2,1)} copy(bf16[1,128,2560]{2,1,0:T(8,128)(2,1)} %bitcast.13) | data formatting | bytes 1310720
  193.4 1.7 copy.19
  195.2 1.7 copy.20
  196.9 1.7 copy.21
  198.6 0.0 copy-done
  198.6 1.7 copy.22
Async XLA Ops:
  1.5 58.6 %copy-start.1 = (s32[1024]{0:T(1024)}, s32[1024]{0:T(1024)S(1)}, u32[]{:S(2)}) copy-start(s32[1024]{0:T(1024)S(1)} %convert_reduce_fusion) | copy-start | bytes 12292
  191.3 7.3 %copy-start = (f32[320,2560]{1,0:T(8,128)S(1)}, f32[320,2560]{1,0:T(8,128)}, u32[]{:S(2)}) copy-start(f32[320,2560]{1,0:T(8,128)} %get-tuple-element.28) | copy-start | bytes 9830404

commit v2 on v1

v2 whole, which is shorter than its diff:
```python
import functools
import math

import jax
import jax.numpy as jnp
from jax import lax
from jax.experimental import pallas as pl
from jax.experimental.pallas import tpu as pltpu
from jax.sharding import PartitionSpec as P

HEADS = 10
HD = 128
MASKED_SCORE = -1e30
MESH = pl.DeviceIdType.MESH
BF16 = jnp.bfloat16
F32 = jnp.float32
VMEM_BYTES = 56 * 1024 * 1024


def owner_of(head, n):
    slot, place = divmod(head, n)
    if slot and 2 * place + 2 < n:
        place = 2 * place + 2
    return place, slot


def head_in_slot(me, slot, n):
    if slot == 0:
        return me, me < HEADS
    head, valid = 0, False
    for h in range(slot * n, min(HEADS, (slot + 1) * n)):
        place = owner_of(h, n)[0]
        head = jnp.where(me == place, h, head)
        valid = jnp.logical_or(valid, me == place)
    return head, valid


def dot_nt(a, b):
    return lax.dot_general(a, b, (((1,), (1,)), ((), ())), preferred_element_type=F32)


def dot_tn(a, b):
    return lax.dot_general(a, b, (((0,), (0,)), ((), ())), preferred_element_type=F32)


def dot_nn(a, b):
    return jnp.dot(a, b, preferred_element_type=F32)


def remote(src, dst, send, recv, dp, ctx):
    return pltpu.make_async_remote_copy(
        src_ref=src, dst_ref=dst, send_sem=send, recv_sem=recv, device_id=(dp, ctx), device_id_type=MESH
    )


def greet(n, ndp):
    me, dp = lax.axis_index("ctx"), lax.axis_index("dp")
    barrier = pltpu.get_barrier_semaphore()
    for step in range(1, n):
        pl.semaphore_signal(barrier, inc=1, device_id=(dp, lax.rem(me + step, n)), device_id_type=MESH)
    for step in range(1, ndp):
        pl.semaphore_signal(barrier, inc=1, device_id=(lax.rem(dp + step, ndp), me), device_id_type=MESH)
    pl.semaphore_wait(barrier, n - 1 + ndp - 1)


def whole_kernel(
    n, ndp, parts, block,
    q_ref, k_ref, v_ref, og_ref, w_ref, seg_col_ref, seg_row_ref,
    attended_ref, qg_ref, kg_ref, vg_ref, wg_ref,
    heads_ref, full_ref, grad_ref, result_ref, norm_ref, key_sum, value_sum,
    att_ref, att_t, xsend_buf, xrecv_buf, csum, rbuf, hsum, zbuf, final,
    send_sem, recv_sem, wsend, wrecv, gsend, grecv,
    hsend, hrecv, xsend, xrecv, rsend, rrecv, zsend, zrecv, bsend, brecv, fsend, frecv,
):
    me, dp = lax.axis_index("ctx"), lax.axis_index("dp")
    core = lax.rem(me, 2)
    chip = me // 2
    chips = n // 2
    sibling = me + 1 - 2 * core
    slots, _, seq, _ = heads_ref.shape
    rows = q_ref.shape[0]
    width = og_ref.shape[1]
    wrows = w_ref.shape[0]
    half = wrows // 2
    wide = width // parts
    scale = 1.0 / math.sqrt(HD)
    my_rows = pl.ds(pl.multiple_of(me * rows, rows), rows)
    greet(n, ndp)

    def weight_rows(owner, which):
        return pl.ds(pl.multiple_of(owner * wrows + which * half, 16), half)

    weight_copies = []
    for step in range(1, ndp):
        copy = remote(
            w_ref.at[pl.ds(pl.multiple_of(core * half, 16), half)],
            full_ref.at[weight_rows(dp, core)],
            wsend.at[step], wrecv.at[step], lax.rem(dp + step, ndp), me,
        )
        copy.start()
        weight_copies.append(copy)

    def send_head(tensor, source, head, start):
        place, slot = owner_of(head, n)
        columns = pl.ds(head * HD, HD)
        copy = remote(
            source.at[:, columns], heads_ref.at[slot, tensor, my_rows],
            send_sem.at[tensor, head], recv_sem.at[slot, tensor], dp, place,
        )

        @pl.when(me != place)
        def _():
            if start:
                copy.start()
            else:
                copy.wait_send()

        if start:
            @pl.when(me == place)
            def _():
                heads_ref[slot, tensor, my_rows, :] = source[:, columns]

    def await_head(slot, tensor):
        waited = heads_ref.at[slot, tensor, pl.ds(0, rows * (n - 1))]
        pltpu.make_async_copy(waited, waited, recv_sem.at[slot, tensor]).wait()

    targets = (att_ref, qg_ref, kg_ref, vg_ref)

    def home_copy(slot, tensor, step):
        head, _ = head_in_slot(me, slot, n)
        other = lax.rem(me + step, n)
        columns = pl.ds(pl.multiple_of(head * HD, HD), HD)
        source = result_ref.at[slot, tensor, pl.ds(pl.multiple_of(other * rows, rows), rows)]
        return remote(
            source, targets[tensor].at[:, columns],
            hsend.at[tensor, slot, step], hrecv.at[tensor, head], dp, other,
        )

    def send_home(slot, tensor):
        head, _ = head_in_slot(me, slot, n)
        for step in range(1, n):
            home_copy(slot, tensor, step).start()
        columns = pl.ds(pl.multiple_of(head * HD, HD), HD)
        targets[tensor][:, columns] = result_ref[slot, tensor, my_rows, :]

    def receive_home(tensor):
        for head in range(HEADS):
            place, _ = owner_of(head, n)

            @pl.when(me != place)
            def _():
                landed = targets[tensor].at[:, pl.ds(head * HD, HD)]
                remote(landed, landed, hsend.at[tensor, 0, 0], hrecv.at[tensor, head], dp, place).wait_recv()

    for tensor, source in enumerate((q_ref, k_ref, v_ref)):
        for head in range(HEADS):
            send_head(tensor, source, head, True)
    full_ref[pl.ds(pl.multiple_of(dp * wrows, 16), wrows), :] = w_ref[...]

    def block_scores(slot, span):
        seen = seg_col_ref[span, :] == seg_row_ref[...]
        scores = dot_nt(heads_ref[slot, 0, span, :], heads_ref[slot, 1]) * scale
        return jnp.where(seen, scores, MASKED_SCORE)

    for slot in range(slots):
        @pl.when(head_in_slot(me, slot, n)[1])
        def _():
            for tensor in range(3):
                await_head(slot, tensor)

            @pl.loop(0, seq // block)
            def _(index):
                span = pl.ds(pl.multiple_of(index * block, block), block)
                scores = block_scores(slot, span)
                top = jnp.max(scores, axis=1, keepdims=True)
                shifted = jnp.exp(scores - top)
                total = jnp.sum(shifted, axis=1, keepdims=True)
                norm_ref[slot, span, :] = top + jnp.log(total)
                probs_b = (shifted * (1.0 / total)).astype(BF16)
                result_ref[slot, 0, span, :] = dot_nn(probs_b, heads_ref[slot, 2]).astype(BF16)

            send_home(slot, 0)

    passes = []
    for step in range(1, ndp):
        weight_copies[step - 1].wait_recv()
        source = lax.rem(dp - step + ndp, ndp)
        landed = full_ref.at[weight_rows(source, core)]
        copy = remote(landed, landed, gsend.at[step], grecv.at[step], dp, sibling)
        copy.start()
        passes.append(copy)
    for copy in passes:
        copy.wait_recv()
    for head in range(HEADS):
        columns = pl.ds(head * HD, HD)
        grad_ref[:, columns] = dot_nt(og_ref[...], full_ref[columns, :]).astype(BF16)
        send_head(3, grad_ref, head, True)

    receive_home(0)
    att_t[...] = att_ref[...].T

    def share(owner, which):
        return pl.multiple_of(owner * 2 * half + which * half, 16)

    def part_columns(part):
        return pl.ds(part * wide, wide)

    def owner_at(step):
        return lax.rem(dp + step + 1, ndp)

    def pair_copy(part, step):
        columns = part_columns(part)
        return remote(
            xsend_buf.at[step, :, columns], xrecv_buf.at[step, :, columns],
            xsend.at[step, part], xrecv.at[step, part], dp, sibling,
        )

    def dp_copy(part, step):
        columns = part_columns(part)
        return remote(
            csum.at[step, :, columns], rbuf.at[step, :, columns],
            rsend.at[step, part], rrecv.at[step, part], owner_at(step), me,
        )

    for part in range(parts):
        columns = part_columns(part)
        for step in range(ndp):
            left = att_t[pl.ds(share(owner_at(step), 1 - core), half), :]
            xsend_buf[step, :, columns] = dot_nn(left, og_ref[:, columns]).astype(BF16)
            pair_copy(part, step).start()
    for part in range(parts):
        columns = part_columns(part)
        for step in range(ndp):
            left = att_t[pl.ds(share(owner_at(step), core), half), :]
            mine = dot_nn(left, og_ref[:, columns])
            pair_copy(part, step).wait_recv()
            csum[step, :, columns] = (mine + xrecv_buf[step, :, columns].astype(F32)).astype(BF16)
            if step < ndp - 1:
                dp_copy(part, step).start()

    for slot in range(slots):
        @pl.when(head_in_slot(me, slot, n)[1])
        def _():
            await_head(slot, 3)
            key_sum[...] = jnp.zeros_like(key_sum)
            value_sum[...] = jnp.zeros_like(value_sum)

            @pl.loop(0, seq // block)
            def _(index):
                span = pl.ds(pl.multiple_of(index * block, block), block)
                grad = heads_ref[slot, 3, span, :]
                probs = jnp.exp(block_scores(slot, span) - norm_ref[slot, span, :])
                attention = result_ref[slot, 0, span, :]
                grad_dot = jnp.sum(grad.astype(F32) * attention.astype(F32), axis=1, keepdims=True)
                dscore = (probs * (dot_nt(grad, heads_ref[slot, 2]) - grad_dot)).astype(BF16)
                result_ref[slot, 1, span, :] = (dot_nn(dscore, heads_ref[slot, 1]) * scale).astype(BF16)
                key_sum[...] += dot_tn(dscore, heads_ref[slot, 0, span, :])
                value_sum[...] += dot_tn(probs.astype(BF16), grad)

            result_ref[slot, 2] = (key_sum[...] * scale).astype(BF16)
            result_ref[slot, 3] = value_sum[...].astype(BF16)
            for tensor in range(1, 4):
                send_home(slot, tensor)

    @pl.loop(0, width // 512)
    def _(index):
        columns = pl.ds(pl.multiple_of(index * 512, 512), 512)
        attended_ref[:, columns] = dot_nn(att_ref[...], full_ref[:, columns]).astype(BF16)

    my_half = pl.ds(pl.multiple_of(core * half, 16), half)
    their_half = pl.ds(pl.multiple_of((1 - core) * half, 16), half)

    def sum_copy(part):
        return remote(
            hsum.at[:, part_columns(part)], zbuf.at[chip],
            zsend.at[part], zrecv.at[chip], dp, 2 * part + core,
        )

    def spread_copy(part, other):
        landed = final.at[my_half, part_columns(part)]
        return remote(landed, landed, bsend.at[other], brecv.at[part], dp, 2 * other + core)

    def pass_copy(part, span):
        landed = final.at[span, part_columns(part)]
        return remote(landed, landed, fsend.at[part], frecv.at[part], dp, sibling)

    def finish(part):
        @pl.when(chip == part)
        def _():
            total = hsum[:, part_columns(part)].astype(F32)
            for other in range(chips):
                if other != part:
                    landed = zbuf.at[other]
                    remote(landed, landed, zsend.at[0], zrecv.at[other], dp, 2 * other + core).wait_recv()
                    total = total + zbuf[other].astype(F32)
            final[my_half, part_columns(part)] = total.astype(BF16)
            for other in range(chips):
                if other != part:
                    spread_copy(part, other).start()

    for part in range(parts):
        columns = part_columns(part)
        total = csum[ndp - 1, :, columns].astype(F32)
        for step in range(ndp - 1):
            dp_copy(part, step).wait_recv()
            total = total + rbuf[step, :, columns].astype(F32)
        hsum[:, columns] = total.astype(BF16)

        @pl.when(chip != part)
        def _():
            sum_copy(part).start()

        if part:
            finish(part - 1)
    finish(parts - 1)

    for part in range(parts):
        @pl.when(chip != part)
        def _():
            spread_copy(part, part).wait_recv()

        pass_copy(part, my_half).start()
    for part in range(parts):
        pass_copy(part, their_half).wait_recv()
    wg_ref[...] = final[...].astype(F32)

    for tensor in range(1, 4):
        receive_home(tensor)
    for tensor, source in enumerate((q_ref, k_ref, v_ref, grad_ref)):
        for head in range(HEADS):
            send_head(tensor, source, head, False)
    for copy in weight_copies + passes:
        copy.wait_send()
    for slot in range(slots):
        @pl.when(head_in_slot(me, slot, n)[1])
        def _():
            for tensor in range(4):
                for step in range(1, n):
                    home_copy(slot, tensor, step).wait_send()
    for part in range(parts):
        for step in range(ndp):
            pair_copy(part, step).wait_send()
            if step < ndp - 1:
                dp_copy(part, step).wait_send()
        pass_copy(part, my_half).wait_send()

        @pl.when(chip != part)
        def _():
            sum_copy(part).wait_send()

        @pl.when(chip == part)
        def _():
            for other in range(chips):
                if other != part:
                    spread_copy(part, other).wait_send()


def copy_kernel(*refs):
    count = len(refs) // 2
    sems = refs[-1]
    copies = [pltpu.make_async_copy(refs[i], refs[count + i], sems.at[i]) for i in range(count)]
    for copy in copies:
        copy.start()
    for copy in copies:
        copy.wait()


def segment_ids(length_row, row_total):
    order = lax.iota(jnp.int32, length_row.shape[0])
    segment_ends = jnp.sum(jnp.where(order[None, :] <= order[:, None], length_row[None, :], 0), axis=1)
    positions = lax.iota(jnp.int32, row_total)
    return jnp.sum((segment_ends[None, :] <= positions[:, None]).astype(jnp.int32), axis=1)


def vmem(count):
    return [pl.BlockSpec(memory_space=pltpu.VMEM)] * count


def local(queries, keys, values, seg_lengths, out_grad, w_out):
    n, ndp = lax.axis_size("ctx"), lax.axis_size("dp")
    rows, inner = queries.shape[1:]
    width = out_grad.shape[2]
    seq = rows * n
    wrows = w_out.shape[0]
    half = wrows // 2
    slots = -(-HEADS // n)
    parts = math.gcd(n // 2, width // 128)
    wide = width // parts
    shape = jax.ShapeDtypeStruct
    dma = pltpu.SemaphoreType.DMA
    segments = segment_ids(seg_lengths[0], seq)
    out_shape = (
        shape((rows, width), BF16), shape((rows, inner), BF16), shape((rows, inner), BF16),
        shape((rows, inner), BF16), shape((wrows, width), F32),
    )
    outputs = pl.pallas_call(
        functools.partial(whole_kernel, n, ndp, parts, 256),
        out_shape=out_shape,
        in_specs=vmem(7),
        out_specs=tuple(vmem(5)),
        scratch_shapes=[
            pltpu.VMEM((slots, 4, seq, HD), BF16),
            pltpu.VMEM((inner, width), BF16),
            pltpu.VMEM((rows, inner), BF16),
            pltpu.VMEM((slots, 4, seq, HD), BF16),
            pltpu.VMEM((slots, seq, 1), F32),
            pltpu.VMEM((seq, HD), F32),
            pltpu.VMEM((seq, HD), F32),
            pltpu.VMEM((rows, inner), BF16),
            pltpu.VMEM((inner, rows), BF16),
            pltpu.VMEM((ndp, half, width), BF16),
            pltpu.VMEM((ndp, half, width), BF16),
            pltpu.VMEM((ndp, half, width), BF16),
            pltpu.VMEM((ndp - 1, half, width), BF16),
            pltpu.VMEM((half, width), BF16),
            pltpu.VMEM((n // 2, half, wide), BF16),
            pltpu.VMEM((wrows, width), BF16),
            dma((4, HEADS)), dma((slots, 4)), dma((ndp,)), dma((ndp,)), dma((ndp,)), dma((ndp,)),
            dma((4, slots, n)), dma((4, HEADS)),
            dma((ndp, parts)), dma((ndp, parts)), dma((ndp, parts)), dma((ndp, parts)),
            dma((parts,)), dma((n // 2,)), dma((n // 2,)), dma((parts,)), dma((parts,)), dma((parts,)),
        ],
        compiler_params=pltpu.CompilerParams(
            collective_id=0, has_side_effects=True, vmem_limit_bytes=VMEM_BYTES
        ),
    )(queries[0], keys[0], values[0], out_grad[0], w_out, segments[:, None], segments[None, :])
    anywhere = [pl.BlockSpec(memory_space=pl.ANY)] * 5
    attended, query_grad, key_grad, value_grad, weight_grad = pl.pallas_call(
        copy_kernel,
        out_shape=out_shape,
        in_specs=anywhere,
        out_specs=tuple(anywhere),
        scratch_shapes=[dma((5,))],
    )(*outputs)
    return (attended[None], query_grad[None], key_grad[None], value_grad[None], weight_grad)


def solution(mesh):
    in_specs = (
        P("dp", "ctx", None),
        P("dp", "ctx", None),
        P("dp", "ctx", None),
        P("dp", None),
        P("dp", "ctx", None),
        P("dp", None),
    )
    out_specs = (
        P("dp", "ctx", None),
        P("dp", "ctx", None),
        P("dp", "ctx", None),
        P("dp", "ctx", None),
        P("dp", None),
    )
    return jax.shard_map(local, mesh=mesh, in_specs=in_specs, out_specs=out_specs, check_vma=False)
```

time: 201 us -> 303 us (1.51)
  Pallas kernels: 189 us -> 300 us
  local copies, waits for them, and re-layouts: 10 us -> 1.03 us
    pallas_call x3 -> x2, Pallas kernels: 189 us -> 300 us  [the longest x1 150 us: local(): pl.pallas_call(copy_kernel, out_shape=out_shape, in_specs=anywhere, out_s...]
    unnamed x9 -> x2, local copies, waits for them, and re-layouts: 8.98 us -> 0.01 us
where the time goes in v2:
time: 303 us
  Pallas kernels  300 us (99%)
    pallas_call x1, Pallas kernels, local(): pl.pallas_call(copy_kernel, out_shape=out_shape, in_specs=anywhere, out_s...  150 us
    pallas_call x1, Pallas kernels, local(): pl.pallas_call(functools.partial(whole_kernel, n, ndp, parts, 256), out_s...  150 us

profile of v2, /device:TPU:17, one launch (start us, length us, event | category | flops | bytes accessed | tf_op | source)
XLA Modules:
  0.0 302.5 jit_solution(17548734941760442826)
XLA Ops:
  0.6 0.8 select_reduce_fusion
  1.4 0.1 convert_reduce_fusion
  1.5 0.0 copy-start
  1.5 1.0 copy.12.seg_col_ref
  2.5 0.0 copy-done
  2.5 149.9 %shard_map.101 = (bf16[128,2560]{1,0:T(8,128)(2,1)}, bf16[128,1280]{1,0:T(8,128)(2,1)}, bf16[128,1280]{1,0:T(8,128)(2,1)}, bf16[128,1280]{1,0:T(8,128)(2,1)}, f32[320,2560]{1,0:T(8,128)}) custom-call(bf16[128,1280]{1,0:T(8,128)(2,1)} %bitcast.12, bf16[128,1280]{1,0:T(8,128)(2,1)} %bitcast.13, bf16[128,1280]{1,0:T(8,128)(2,1)} %bitcast.14, ...), custom_call_target="tpu_custom_call" | custom-call | tf_op jit(solution)/shard_map/pallas_call | solution.py:396
  152.5 150.0 %shard_map.102 = (bf16[128,2560]{1,0:T(8,128)(2,1)}, bf16[128,1280]{1,0:T(8,128)(2,1)}, bf16[128,1280]{1,0:T(8,128)(2,1)}, bf16[128,1280]{1,0:T(8,128)(2,1)}, f32[320,2560]{1,0:T(8,128)}) custom-call(bf16[128,2560]{1,0:T(8,128)(2,1)} %get-tuple-element.15.refs_0_, bf16[128,1280]{1,0:T(8,128)(2,1)} %get-tuple-element.16.refs_1_, ...), custom_call_target="tpu_custom_call" | custom-call | tf_op jit(solution)/shard_map/pallas_call | solution.py:428
Async XLA Ops:
  1.5 1.0 copy-start

commit v3 on v2

--- a/solution.py
+++ b/solution.py
@@ -68,7 +68,7 @@
     q_ref, k_ref, v_ref, og_ref, w_ref, seg_col_ref, seg_row_ref,
     attended_ref, qg_ref, kg_ref, vg_ref, wg_ref,
     heads_ref, full_ref, grad_ref, result_ref, norm_ref, key_sum, value_sum,
-    att_ref, att_t, xsend_buf, xrecv_buf, csum, rbuf, hsum, zbuf, final,
+    att_ref, att_t, xsend_buf, xrecv_buf, csum, rbuf, hsum, zbuf, acc, final,
     send_sem, recv_sem, wsend, wrecv, gsend, grecv,
     hsend, hrecv, xsend, xrecv, rsend, rrecv, zsend, zrecv, bsend, brecv, fsend, frecv,
 ):
@@ -181,6 +181,38 @@
 
             send_home(slot, 0)
 
+    receive_home(0)
+    att_t[...] = att_ref[...].T
+
+    def share(owner, which):
+        return pl.multiple_of(owner * 2 * half + which * half, 16)
+
+    def part_columns(part):
+        return pl.ds(part * wide, wide)
+
+    def owner_at(step):
+        return lax.rem(dp + step + 1, ndp)
+
+    def pair_copy(part, step):
+        columns = part_columns(part)
+        return remote(
+            xsend_buf.at[step, :, columns], xrecv_buf.at[step, :, columns],
+            xsend.at[step, part], xrecv.at[step, part], dp, sibling,
+        )
+
+    def dp_copy(part, step):
+        columns = part_columns(part)
+        return remote(
+            csum.at[step, :, columns], rbuf.at[step, :, columns],
+            rsend.at[step, part], rrecv.at[step, part], owner_at(step), me,
+        )
+
+    for part in range(parts):
+        columns = part_columns(part)
+        for step in range(ndp):
+            left = att_t[pl.ds(share(owner_at(step), 1 - core), half), :]
+            xsend_buf[step, :, columns] = dot_nn(left, og_ref[:, columns]).astype(BF16)
+            pair_copy(part, step).start()
     passes = []
     for step in range(1, ndp):
         weight_copies[step - 1].wait_recv()
@@ -196,38 +228,6 @@
         grad_ref[:, columns] = dot_nt(og_ref[...], full_ref[columns, :]).astype(BF16)
         send_head(3, grad_ref, head, True)
 
-    receive_home(0)
-    att_t[...] = att_ref[...].T
-
-    def share(owner, which):
-        return pl.multiple_of(owner * 2 * half + which * half, 16)
-
-    def part_columns(part):
-        return pl.ds(part * wide, wide)
-
-    def owner_at(step):
-        return lax.rem(dp + step + 1, ndp)
-
-    def pair_copy(part, step):
-        columns = part_columns(part)
-        return remote(
-            xsend_buf.at[step, :, columns], xrecv_buf.at[step, :, columns],
-            xsend.at[step, part], xrecv.at[step, part], dp, sibling,
-        )
-
-    def dp_copy(part, step):
-        columns = part_columns(part)
-        return remote(
-            csum.at[step, :, columns], rbuf.at[step, :, columns],
-            rsend.at[step, part], rrecv.at[step, part], owner_at(step), me,
-        )
-
-    for part in range(parts):
-        columns = part_columns(part)
-        for step in range(ndp):
-            left = att_t[pl.ds(share(owner_at(step), 1 - core), half), :]
-            xsend_buf[step, :, columns] = dot_nn(left, og_ref[:, columns]).astype(BF16)
-            pair_copy(part, step).start()
     for part in range(parts):
         columns = part_columns(part)
         for step in range(ndp):
@@ -270,59 +270,75 @@
     my_half = pl.ds(pl.multiple_of(core * half, 16), half)
     their_half = pl.ds(pl.multiple_of((1 - core) * half, 16), half)
 
-    def sum_copy(part):
+    right, left_side = lax.rem(me + 2, n), lax.rem(me + n - 2, n)
+
+    def goes_left(part):
+        return jnp.logical_and(chip > 0, chip <= part)
+
+    def goes_right(part):
+        return jnp.logical_and(chip < chips - 1, chip >= part)
+
+    def sum_copy(part, side):
         return remote(
-            hsum.at[:, part_columns(part)], zbuf.at[chip],
-            zsend.at[part], zrecv.at[chip], dp, 2 * part + core,
-        )
-
-    def spread_copy(part, other):
+            hsum.at[:, part_columns(part)], zbuf.at[side, part],
+            zsend.at[part], zrecv.at[side, part], dp, right if side == 0 else left_side,
+        )
+
+    def spread_copy(part, side):
         landed = final.at[my_half, part_columns(part)]
-        return remote(landed, landed, bsend.at[other], brecv.at[part], dp, 2 * other + core)
+        return remote(
+            landed, landed, bsend.at[part, side], brecv.at[part], dp, left_side if side == 0 else right
+        )
 
     def pass_copy(part, span):
         landed = final.at[span, part_columns(part)]
         return remote(landed, landed, fsend.at[part], frecv.at[part], dp, sibling)
 
-    def finish(part):
-        @pl.when(chip == part)
-        def _():
-            total = hsum[:, part_columns(part)].astype(F32)
-            for other in range(chips):
-                if other != part:
-                    landed = zbuf.at[other]
-                    remote(landed, landed, zsend.at[0], zrecv.at[other], dp, 2 * other + core).wait_recv()
-                    total = total + zbuf[other].astype(F32)
-            final[my_half, part_columns(part)] = total.astype(BF16)
-            for other in range(chips):
-                if other != part:
-                    spread_copy(part, other).start()
-
-    for part in range(parts):
+    def reduce_part(part):
         columns = part_columns(part)
         total = csum[ndp - 1, :, columns].astype(F32)
         for step in range(ndp - 1):
             dp_copy(part, step).wait_recv()
             total = total + rbuf[step, :, columns].astype(F32)
-        hsum[:, columns] = total.astype(BF16)
-
+        acc[...] = total
+        for side, comes in ((0, goes_left(part)), (1, goes_right(part))):
+            @pl.when(comes)
+            def _():
+                sum_copy(part, side).wait_recv()
+                acc[...] += zbuf[side, part].astype(F32)
+
+        for side, onward in ((0, chip < part), (1, chip > part)):
+            @pl.when(onward)
+            def _():
+                hsum[:, columns] = acc[...].astype(BF16)
+                sum_copy(part, side).start()
+
+        @pl.when(chip == part)
+        def _():
+            final[my_half, columns] = acc[...].astype(BF16)
+
+    def spread_part(part):
         @pl.when(chip != part)
         def _():
-            sum_copy(part).start()
-
-        if part:
-            finish(part - 1)
-    finish(parts - 1)
-
-    for part in range(parts):
-        @pl.when(chip != part)
-        def _():
-            spread_copy(part, part).wait_recv()
+            spread_copy(part, 0).wait_recv()
+
+        for side, onward in ((0, goes_left(part)), (1, goes_right(part))):
+            @pl.when(onward)
+            def _():
+                spread_copy(part, side).start()
 
         pass_copy(part, my_half).start()
+
+    order = (0, 3, 1, 2) if parts == 4 else tuple(range(parts))
+    for turn, part in enumerate(order):
+        reduce_part(part)
+        if turn > 1:
+            spread_part(order[turn - 2])
+    for part in order[max(0, parts - 2):]:
+        spread_part(part)
     for part in range(parts):
         pass_copy(part, their_half).wait_recv()
-    wg_ref[...] = final[...].astype(F32)
+    wg_ref[...] = final[...]
 
     for tensor in range(1, 4):
         receive_home(tensor)
@@ -346,23 +362,31 @@
 
         @pl.when(chip != part)
         def _():
-            sum_copy(part).wait_send()
-
-        @pl.when(chip == part)
-        def _():
-            for other in range(chips):
-                if other != part:
-                    spread_copy(part, other).wait_send()
+            sum_copy(part, 0).wait_send()
+
+        for side, onward in ((0, goes_left(part)), (1, goes_right(part))):
+            @pl.when(onward)
+            def _():
+                spread_copy(part, side).wait_send()
 
 
 def copy_kernel(*refs):
-    count = len(refs) // 2
-    sems = refs[-1]
-    copies = [pltpu.make_async_copy(refs[i], refs[count + i], sems.at[i]) for i in range(count)]
-    for copy in copies:
-        copy.start()
-    for copy in copies:
-        copy.wait()
+    sources, targets, held = refs[:5], refs[5:10], refs[10:15]
+    wide_held, in_sem, out_sem = refs[15:]
+    loads = [pltpu.make_async_copy(sources[i], held[i], in_sem.at[i]) for i in range(5)]
+    stores = [
+        pltpu.make_async_copy(held[i] if i < 4 else wide_held, targets[i], out_sem.at[i]) for i in range(5)
+    ]
+    for i in (4, 0, 1, 2, 3):
+        loads[i].start()
+    loads[4].wait()
+    wide_held[...] = held[4][...].astype(F32)
+    stores[4].start()
+    for i in range(4):
+        loads[i].wait()
+        stores[i].start()
+    for store in stores:
+        store.wait()
 
 
 def segment_ids(length_row, row_total):
@@ -395,7 +419,7 @@
     )
     outputs = pl.pallas_call(
         functools.partial(whole_kernel, n, ndp, parts, 256),
-        out_shape=out_shape,
+        out_shape=out_shape[:4] + (shape((wrows, width), BF16),),
         in_specs=vmem(7),
         out_specs=tuple(vmem(5)),
         scratch_shapes=[
@@ -413,12 +437,13 @@
             pltpu.VMEM((ndp, half, width), BF16),
             pltpu.VMEM((ndp - 1, half, width), BF16),
             pltpu.VMEM((half, width), BF16),
-            pltpu.VMEM((n // 2, half, wide), BF16),
+            pltpu.VMEM((2, parts, half, wide), BF16),
+            pltpu.VMEM((half, wide), F32),
             pltpu.VMEM((wrows, width), BF16),
             dma((4, HEADS)), dma((slots, 4)), dma((ndp,)), dma((ndp,)), dma((ndp,)), dma((ndp,)),
             dma((4, slots, n)), dma((4, HEADS)),
             dma((ndp, parts)), dma((ndp, parts)), dma((ndp, parts)), dma((ndp, parts)),
-            dma((parts,)), dma((n // 2,)), dma((n // 2,)), dma((parts,)), dma((parts,)), dma((parts,)),
+            dma((parts,)), dma((2, parts)), dma((parts, 2)), dma((parts,)), dma((parts,)), dma((parts,)),
         ],
         compiler_params=pltpu.CompilerParams(
             collective_id=0, has_side_effects=True, vmem_limit_bytes=VMEM_BYTES
@@ -430,7 +455,9 @@
         out_shape=out_shape,
         in_specs=anywhere,
         out_specs=tuple(anywhere),
-        scratch_shapes=[dma((5,))],
+        scratch_shapes=[pltpu.VMEM(x.shape, BF16) for x in out_shape]
+        + [pltpu.VMEM((wrows, width), F32), dma((5,)), dma((5,))],
+        compiler_params=pltpu.CompilerParams(vmem_limit_bytes=VMEM_BYTES),
     )(*outputs)
     return (attended[None], query_grad[None], key_grad[None], value_grad[None], weight_grad)
 

time: 303 us -> 171 us (0.56)
  the two profiles are of different devices: /device:TPU:17 before, /device:TPU:1 now
where the time goes in v3:
time: 171 us
  Pallas kernels  169 us (99%)
    pallas_call x1, Pallas kernels, local(): pl.pallas_call(functools.partial(whole_kernel, n, ndp, parts, 256), out_s...  165 us
    pallas_call x1, Pallas kernels, local(): pl.pallas_call(copy_kernel, out_shape=out_shape, in_specs=anywhere, out_s...  3.96 us

profile of v3, /device:TPU:1, one launch (start us, length us, event | category | flops | bytes accessed | tf_op | source)
XLA Modules:
  0.0 171.3 jit_solution(4684652858645318682)
XLA Ops:
  0.6 0.8 select_reduce_fusion
  1.4 0.1 convert_reduce_fusion
  1.5 0.0 copy-start
  1.5 1.0 copy.12.seg_col_ref
  2.5 0.0 copy-done
  2.5 164.8 %shard_map.101 = (bf16[128,2560]{1,0:T(8,128)(2,1)}, bf16[128,1280]{1,0:T(8,128)(2,1)}, bf16[128,1280]{1,0:T(8,128)(2,1)}, bf16[128,1280]{1,0:T(8,128)(2,1)}, bf16[320,2560]{1,0:T(8,128)(2,1)}) custom-call(bf16[128,1280]{1,0:T(8,128)(2,1)} %bitcast.12, bf16[128,1280]{1,0:T(8,128)(2,1)} %bitcast.13, bf16[128,1280]{1,0:T(8,128)(2,1)} %bitcast.14, ...), custom_call_target="tpu_custom_call" | custom-call | tf_op jit(solution)/shard_map/pallas_call | solution.py:420
  167.3 4.0 %shard_map.102 = (bf16[128,2560]{1,0:T(8,128)(2,1)}, bf16[128,1280]{1,0:T(8,128)(2,1)}, bf16[128,1280]{1,0:T(8,128)(2,1)}, bf16[128,1280]{1,0:T(8,128)(2,1)}, f32[320,2560]{1,0:T(8,128)}) custom-call(bf16[128,2560]{1,0:T(8,128)(2,1)} %get-tuple-element.15.refs_0_, bf16[128,1280]{1,0:T(8,128)(2,1)} %get-tuple-element.16.refs_1_, ...), custom_call_target="tpu_custom_call" | custom-call | tf_op jit(solution)/shard_map/pallas_call | solution.py:453
Async XLA Ops:
  1.5 1.0 copy-start

commit v4 on v2

--- a/solution.py
+++ b/solution.py
@@ -322,7 +322,7 @@
         pass_copy(part, my_half).start()
     for part in range(parts):
         pass_copy(part, their_half).wait_recv()
-    wg_ref[...] = final[...].astype(F32)
+    wg_ref[...] = final[...]
 
     for tensor in range(1, 4):
         receive_home(tensor)
@@ -356,13 +356,22 @@
 
 
 def copy_kernel(*refs):
-    count = len(refs) // 2
-    sems = refs[-1]
-    copies = [pltpu.make_async_copy(refs[i], refs[count + i], sems.at[i]) for i in range(count)]
-    for copy in copies:
-        copy.start()
-    for copy in copies:
-        copy.wait()
+    sources, targets, held = refs[:5], refs[5:10], refs[10:15]
+    wide_held, in_sem, out_sem = refs[15:]
+    loads = [pltpu.make_async_copy(sources[i], held[i], in_sem.at[i]) for i in range(5)]
+    stores = [
+        pltpu.make_async_copy(held[i] if i < 4 else wide_held, targets[i], out_sem.at[i]) for i in range(5)
+    ]
+    for i in (4, 0, 1, 2, 3):
+        loads[i].start()
+    loads[4].wait()
+    wide_held[...] = held[4][...].astype(F32)
+    stores[4].start()
+    for i in range(4):
+        loads[i].wait()
+        stores[i].start()
+    for store in stores:
+        store.wait()
 
 
 def segment_ids(length_row, row_total):
@@ -395,7 +404,7 @@
     )
     outputs = pl.pallas_call(
         functools.partial(whole_kernel, n, ndp, parts, 256),
-        out_shape=out_shape,
+        out_shape=out_shape[:4] + (shape((wrows, width), BF16),),
         in_specs=vmem(7),
         out_specs=tuple(vmem(5)),
         scratch_shapes=[
@@ -430,7 +439,9 @@
         out_shape=out_shape,
         in_specs=anywhere,
         out_specs=tuple(anywhere),
-        scratch_shapes=[dma((5,))],
+        scratch_shapes=[pltpu.VMEM(x.shape, BF16) for x in out_shape]
+        + [pltpu.VMEM((wrows, width), F32), dma((5,)), dma((5,))],
+        compiler_params=pltpu.CompilerParams(vmem_limit_bytes=VMEM_BYTES),
     )(*outputs)
     return (attended[None], query_grad[None], key_grad[None], value_grad[None], weight_grad)
 

time: 303 us -> 156 us (0.51)
  Pallas kernels: 300 us -> 153 us
    pallas_call x1, Pallas kernels: 150 us -> 3.96 us  [local(): pl.pallas_call(copy_kernel, out_shape=out_shape, in_specs=anywhere, out_s...]
where the time goes in v4:
time: 156 us
  Pallas kernels  153 us (98%)
    pallas_call x1, Pallas kernels, local(): pl.pallas_call(functools.partial(whole_kernel, n, ndp, parts, 256), out_s...  149 us
    pallas_call x1, Pallas kernels, local(): pl.pallas_call(copy_kernel, out_shape=out_shape, in_specs=anywhere, out_s...  3.96 us

profile of v4, /device:TPU:17, one launch (start us, length us, event | category | flops | bytes accessed | tf_op | source)
XLA Modules:
  0.0 155.9 jit_solution(5235571205312527343)
XLA Ops:
  0.6 0.8 select_reduce_fusion
  1.4 0.1 convert_reduce_fusion
  1.5 0.0 copy-start
  1.5 1.0 copy.12.seg_col_ref
  2.5 0.0 copy-done
  2.5 149.4 %shard_map.101 = (bf16[128,2560]{1,0:T(8,128)(2,1)}, bf16[128,1280]{1,0:T(8,128)(2,1)}, bf16[128,1280]{1,0:T(8,128)(2,1)}, bf16[128,1280]{1,0:T(8,128)(2,1)}, bf16[320,2560]{1,0:T(8,128)(2,1)}) custom-call(bf16[128,1280]{1,0:T(8,128)(2,1)} %bitcast.12, bf16[128,1280]{1,0:T(8,128)(2,1)} %bitcast.13, bf16[128,1280]{1,0:T(8,128)(2,1)} %bitcast.14, ...), custom_call_target="tpu_custom_call" | custom-call | tf_op jit(solution)/shard_map/pallas_call | solution.py:405
  152.0 4.0 %shard_map.102 = (bf16[128,2560]{1,0:T(8,128)(2,1)}, bf16[128,1280]{1,0:T(8,128)(2,1)}, bf16[128,1280]{1,0:T(8,128)(2,1)}, bf16[128,1280]{1,0:T(8,128)(2,1)}, f32[320,2560]{1,0:T(8,128)}) custom-call(bf16[128,2560]{1,0:T(8,128)(2,1)} %get-tuple-element.15.refs_0_, bf16[128,1280]{1,0:T(8,128)(2,1)} %get-tuple-element.16.refs_1_, ...), custom_call_target="tpu_custom_call" | custom-call | tf_op jit(solution)/shard_map/pallas_call | solution.py:437
Async XLA Ops:
  1.5 1.0 copy-start
